TPU v7x, 32 devices: a whole 2x2x4 slice. The times are simulated.
32 devices in a mesh: tile: 16 (over z, y, core), grp: 2 (over x).
Axes of the slice: x: 2, y: 2, z: 4, core: 2. Of those that a mesh axis runs over, the one named last changes fastest.
Arguments:
- points: bfloat16 [4096, 256], P(('tile', 'grp')), may hold values from -6 to 6
- targets: bfloat16 [4096], P(('tile', 'grp')), may hold values from -12 to 12
- morton: int32 [4096], P(('tile', 'grp')), may hold values from 0 to 15, as said below
- inducing: bfloat16 [8192, 256], P('tile'), may hold values from -6 to 6
- means: bfloat16 [8192], P('tile'), may hold values from -6 to 6
- scales: bfloat16 [8192], P('tile'), may hold values from 0.099609375 to 1.3984375
- neighbours: int32 [16, 8], replicated, may hold values from 0 to 63, as said below
Outputs:
- grad_inducing: float32 [8192, 256], P(('tile', 'grp'))
- grad_means: float32 [8192], P(('tile', 'grp'))
- grad_scales: float32 [8192], P(('tile', 'grp'))
Inputs may be any that keep to these rules, and one draw needn't show every extreme that they name: `morton`: each aligned block of 128 rows names every tile exactly 8 times. `neighbours`: block b is owned by tile b // 4. Row t names only blocks owned by tiles t - 1, t and t + 1; entry 0 is owned by tile t - 1 and entry 1 by tile t + 1 where these exist (else by t), entry 2 by t. Ids may repeat.
All inputs are finite; a program needn't handle non-finite values.
Results may differ from a plain program's by a relative error of at most 0.0003.
Values may be sent and summed in bfloat16 or wider, within the bound.
A program may use at most 64 MiB of HBM per device.

v0:
```python
import math

import jax
import jax.numpy as jnp
from jax import lax
from jax.sharding import PartitionSpec as P

BS = 128


def extended(block, sides, width):
    for axis, dim in sides:
        count = lax.axis_size(axis)
        forward = [(i, i + 1) for i in range(count - 1)]
        backward = [(target, source) for source, target in forward]
        low = lax.ppermute(
            lax.slice_in_dim(block, block.shape[dim] - width, None, axis=dim), axis, forward
        )
        high = lax.ppermute(lax.slice_in_dim(block, 0, width, axis=dim), axis, backward)
        block = jnp.concatenate([low, block, high], axis=dim)
    return block


def passed_along(shard, axis, by):
    count = lax.axis_size(axis)
    pairs = [(i, i + by) for i in range(count) if 0 <= i + by < count]
    return lax.ppermute(shard, axis, pairs)


def distances(feats, feat_sq, block_rows):
    cross = lax.dot_general(
        feats, block_rows, (((1,), (1,)), ((), ())), preferred_element_type=jnp.float32
    )
    block_f = block_rows.astype(jnp.float32)
    block_sq = jnp.sum(block_f * block_f, axis=1)
    dist_sq = feat_sq[:, None] + block_sq[None, :] - 2.0 * cross
    return (dist_sq, block_f)


def wendland(dist_sq, block_scale, width):
    radius = jnp.sqrt(block_scale[None, :] * dist_sq / (2.0 * width))
    remain = 1.0 - jnp.minimum(radius, 1.0)
    value = remain**4 * (4.0 * radius + 1.0)
    slope = -10.0 * remain**3
    return (value, slope)


def add_rows(buffer, start, piece):
    current = lax.dynamic_slice_in_dim(buffer, start, piece.shape[0], 0)
    return lax.dynamic_update_slice_in_dim(buffer, current + piece, start, 0)


def shards(points, targets, morton, inducing, means, scales, neighbours):
    tiles = lax.axis_size("tile")
    groups = lax.axis_size("grp")
    rows, width = points.shape
    per_tile = rows // tiles
    bsize = BS
    owned = inducing.shape[0] // bsize
    order = jnp.argsort(morton, stable=True)
    grouped = jnp.take(points, order, axis=0).reshape(tiles, per_tile, width)
    goals = jnp.take(targets, order, axis=0).reshape(tiles, per_tile)
    arrived, reached = (
        lax.all_to_all(grouped, "tile", split_axis=0, concat_axis=0, tiled=True),
        lax.all_to_all(goals, "tile", split_axis=0, concat_axis=0, tiled=True),
    )
    feats = arrived.reshape(rows, width)
    wanted = reached.reshape(rows).astype(jnp.float32)
    params = jnp.stack([means, scales], axis=1)
    window, wparams = (
        extended(inducing, (("tile", 0),), owned * bsize),
        extended(params, (("tile", 0),), owned * bsize),
    )
    here = lax.axis_index("tile")
    block_ids = lax.dynamic_index_in_dim(neighbours, here, 0, keepdims=False)
    slots = block_ids - (here - 1) * owned
    feat_sq = jnp.sum(jnp.square(feats.astype(jnp.float32)), axis=1)
    count = block_ids.shape[0]

    def pick(slot):
        start = slot * bsize
        rows_k = lax.dynamic_slice_in_dim(window, start, bsize, 0)
        params_k = lax.dynamic_slice_in_dim(wparams, start, bsize, 0).astype(jnp.float32)
        return (start, rows_k, params_k[:, 0], params_k[:, 1])

    estimate = jnp.zeros((rows,), jnp.float32)
    stored = []
    for slot_index in range(count):
        start, rows_k, mean_k, scale_k = pick(slots[slot_index])
        dist_sq, block_f = distances(feats, feat_sq, rows_k)
        value, slope = wendland(dist_sq, scale_k, width)
        estimate = estimate + jnp.dot(value, mean_k, precision=lax.Precision.HIGHEST)
        stored.append((dist_sq, block_f))
    error = estimate - wanted
    total = 3 * owned * bsize
    grad_rows = jnp.zeros((total, width), jnp.float32)
    grad_mean = jnp.zeros((total,), jnp.float32)
    grad_scale = jnp.zeros((total,), jnp.float32)
    for slot_index in range(count):
        start, rows_k, mean_k, scale_k = pick(slots[slot_index])
        dist_sq, block_f = stored[slot_index]
        value, slope = wendland(dist_sq, scale_k, width)
        weight = error[:, None] * mean_k[None, :] * slope
        mean_piece = jnp.dot(error, value, precision=lax.Precision.HIGHEST)
        scale_piece = jnp.sum(weight * dist_sq, axis=0) / (2.0 * width)
        column = jnp.sum(weight, axis=0)
        back = lax.dot_general(
            weight.astype(jnp.bfloat16),
            feats,
            (((0,), (0,)), ((), ())),
            preferred_element_type=jnp.float32,
        )
        row_piece = (scale_k / width)[:, None] * (block_f * column[:, None] - back)
        grad_rows = add_rows(grad_rows, start, row_piece)
        grad_mean = add_rows(grad_mean, start, mean_piece)
        grad_scale = add_rows(grad_scale, start, scale_piece)
    shaped = (
        grad_rows.reshape(3, owned, bsize, width),
        grad_mean.reshape(3, owned, bsize),
        grad_scale.reshape(3, owned, bsize),
    )
    mine = owned // groups
    summed = lax.psum((shaped[0], shaped[1], shaped[2]), "grp")
    result = [part[1] for part in summed]
    for by_value, side in ((1, 2), (-1, 0)):
        moved = passed_along((summed[0][side], summed[1][side], summed[2][side]), "tile", by_value)
        result = [result[index] + moved[index] for index in range(3)]
    first = lax.axis_index("grp") * mine
    result = [lax.dynamic_slice_in_dim(part, first, mine, 0) for part in result]
    norm = 1.0 / math.sqrt(rows * groups)
    return (
        result[0].reshape(mine * bsize, width) * norm,
        result[1].reshape(mine * bsize) * norm,
        result[2].reshape(mine * bsize) * norm,
    )


def solution(mesh):
    placed = (
        P(("tile", "grp"), None),
        P(("tile", "grp")),
        P(("tile", "grp")),
        P("tile", None),
        P("tile"),
        P("tile"),
        P(),
    )
    return jax.shard_map(
        shards,
        mesh=mesh,
        in_specs=placed,
        out_specs=(P(("tile", "grp"), None), P(("tile", "grp")), P(("tile", "grp"))),
        check_vma=False,
    )
```

profile of v0, /device:TPU:1, one launch (start us, length us, event | category | flops | bytes accessed | tf_op | source)
XLA Modules:
  0.0 135.0 jit_solution(14526956415006988592)
XLA Ops:
  7.2 4.7 %collective-permute-start.2 = (bf16[512,256]{1,0:T(8,128)(2,1)}, bf16[512,256]{1,0:T(8,128)(2,1)S(1)}, u32[]{:S(2)}, u32[]{:S(2)}) collective-permute-start(bf16[512,256]{1,0:T(8,128)(2,1)} %param.10), channel_id=1, source_target_pairs={{0,2},{2,4},{4,6},{6,8},{8,10},{10,12},{12,14},{14,16},{16,18},{18... | collective-permute-start | bytes 786440 | tf_op jit(solution)/shard_map/ppermute | solution.py:16
  11.9 1.9 %collective-permute-start.3 = (bf16[512,256]{1,0:T(8,128)(2,1)}, bf16[512,256]{1,0:T(8,128)(2,1)S(1)}, u32[]{:S(2)}, u32[]{:S(2)}) collective-permute-start(bf16[512,256]{1,0:T(8,128)(2,1)} %param.10), channel_id=1, source_target_pairs={{2,0},{4,2},{6,4},{8,6},{10,8},{12,10},{14,12},{16,14},{18,16},{20... | collective-permute-start | bytes 786440 | tf_op jit(solution)/shard_map/ppermute | solution.py:19
  13.8 0.7 stack.10
  14.5 0.7 stack.9
  15.2 1.9 %collective-permute-start.1 = (bf16[512,2]{0,1:T(2,128)(2,1)S(1)}, bf16[512,2]{0,1:T(2,128)(2,1)S(1)}, u32[]{:S(2)}, u32[]{:S(2)}) collective-permute-start(bf16[512,2]{0,1:T(2,128)(2,1)S(1)} %pad_maximum_fusion.1), channel_id=1, source_target_pairs={{2,0},{4,2},{6,4},{8,6},{10,8},{12,10},{14,12},{16,14},{18,16},{20... | collective-permute-start | bytes 6152 | tf_op jit(solution)/shard_map/ppermute | solution.py:19
  17.1 3.6 %collective-permute-start = (bf16[512,2]{0,1:T(2,128)(2,1)S(1)}, bf16[512,2]{0,1:T(2,128)(2,1)S(1)}, u32[]{:S(2)}, u32[]{:S(2)}) collective-permute-start(bf16[512,2]{0,1:T(2,128)(2,1)S(1)} %pad_maximum_fusion.1), channel_id=1, source_target_pairs={{0,2},{2,4},{4,6},{6,8},{8,10},{10,12},{12,14},{14,16},{16,18},{18... | collective-permute-start | bytes 6152 | tf_op jit(solution)/shard_map/ppermute | solution.py:16
  20.8 3.2 %sort.17 = (s32[128]{0:T(128)}, s32[128]{0:T(128)S(1)}) sort(s32[128]{0:T(128)} %param.9, s32[128]{0:T(128)S(1)} %iota.4), dimensions={0}, to_apply=%region_0.0 | sort | flops 896 | bytes 2048 | tf_op jit(solution)/shard_map/jit(argsort)/sort | solution.py:60
  24.0 1.6 %gather_fusion.1 = bf16[128]{0:T(256)(128)(2,1)S(1)} fusion(bf16[128]{0:T(256)(128)(2,1)} %param.8, s32[1024]{0:T(1024)S(1)} %pad_clamp_fusion), kind=kCustom, calls=%fused_computation.1 | custom fusion | bytes 1024 | tf_op jit(solution)/shard_map/jit(_take)/gather | solution.py:62
  25.6 0.7 select_n.63
  26.3 5.8 %all-to-all-start.1 = ((bf16[16,1,8]{2,1,0:T(2,128)(2,1)}), bf16[16,1,8]{2,1,0:T(2,128)(2,1)S(1)}, u32[]{:S(2)}, u32[]{:S(2)}) async-start(bf16[16,1,8]{2,1,0:T(2,128)(2,1)} %select_n.63), calls=%async_computation.1 | async-start | bytes 16384 | tf_op jit(solution)/shard_map/all_to_all | solution.py:65
  32.1 0.8 fusion.167
  32.9 0.6 fusion.264
  38.5 0.8 gather_fusion
  39.5 0.7 bitcast_select_fusion
  40.2 6.0 %all-to-all-start = ((bf16[16,8,256]{2,1,0:T(8,128)(2,1)}), bf16[16,8,256]{2,1,0:T(8,128)(2,1)S(1)}, u32[]{:S(2)}, u32[]{:S(2)}) async-start(bf16[16,8,256]{2,1,0:T(8,128)(2,1)} %bitcast_select_fusion), calls=%async_computation | async-start | bytes 131072 | tf_op jit(solution)/shard_map/all_to_all | solution.py:64
  46.5 5.7 %all-to-all-done = bf16[16,8,256]{2,1,0:T(8,128)(2,1)S(1)} async-done(((bf16[16,8,256]{2,1,0:T(8,128)(2,1)}), bf16[16,8,256]{2,1,0:T(8,128)(2,1)S(1)}, u32[]{:S(2)}, u32[]{:S(2)}) %all-to-all-start) | async-done | bytes 65568 | tf_op jit(solution)/shard_map/all_to_all | solution.py:64
  52.5 0.2 fusion.58
  52.8 0.2 fusion.7
  53.1 0.2 fusion.6
  53.3 0.2 fusion.21
  53.5 0.2 fusion.5
  53.7 0.2 fusion.20
  53.9 0.2 fusion.4
  54.3 0.2 fusion.3
  54.7 0.2 fusion.2
  54.9 0.2 fusion.17
  55.1 0.2 fusion.1
  55.3 0.2 fusion.16
  55.4 0.2 fusion
  55.7 0.2 fusion.22
  55.8 0.2 convolution_bitcast_fusion.7
  56.1 0.2 multiply_reduce_fusion.2
  56.2 0.2 multiply_reduce_fusion.1
  56.6 0.3 fusion.27
  56.9 0.3 fusion.32
  57.2 0.3 fusion.37
  57.4 0.3 fusion.42
  57.7 0.3 fusion.47
  58.0 0.3 fusion.52
  58.3 0.3 fusion.57
  58.6 0.3 fusion.62
  58.8 1.1 copy-done.1
  60.0 0.3 dynamic_update_slice.80
  60.5 0.2 dynamic_update_slice.81
  60.8 0.2 dynamic_update_slice.82
  61.2 0.2 dynamic_update_slice.83
  61.6 0.2 dynamic_update_slice.84
  62.0 0.2 dynamic_update_slice.85
  62.3 0.2 dynamic_update_slice.86
  62.7 0.2 dynamic_update_slice.87
  64.2 7.1 %all-reduce = (f32[3,4,128]{2,1,0:T(4,128)S(1)}, f32[3,4,128]{2,1,0:T(4,128)S(1)}) all-reduce(f32[3,4,128]{2,1,0:T(4,128)S(1)} %reshape.156, f32[3,4,128]{2,1,0:T(4,128)S(1)} %reshape.157), channel_id=1, replica_groups=mesh['tile'=16,'grp'=2] {'grp'}, use_global_device_ids=true, to_apply=%region_19.20 | all-reduce | flops 3072 | bytes 24576 | tf_op jit(solution)/shard_map/psum | solution.py:123
  71.4 4.1 %collective-permute-start.7 = (f32[4,128]{1,0:T(4,128)S(1)}, f32[4,128]{1,0:T(4,128)S(1)}, u32[]{:S(2)}, u32[]{:S(2)}) collective-permute-start(f32[4,128]{1,0:T(4,128)S(1)} %get-tuple-element.67), channel_id=1, source_target_pairs={{2,0},{4,2},{6,4},{8,6},{10,8},{12,10},{14,12},{16,14},{18,16},{20... | collective-permute-start | bytes 6152 | tf_op jit(solution)/shard_map/ppermute | solution.py:27
  75.5 1.9 %collective-permute-start.6 = (f32[4,128]{1,0:T(4,128)S(1)}, f32[4,128]{1,0:T(4,128)S(1)}, u32[]{:S(2)}, u32[]{:S(2)}) collective-permute-start(f32[4,128]{1,0:T(4,128)S(1)} %get-tuple-element.66), channel_id=1, source_target_pairs={{0,2},{2,4},{4,6},{6,8},{8,10},{10,12},{12,14},{14,16},{16,18},{18... | collective-permute-start | bytes 6152 | tf_op jit(solution)/shard_map/ppermute | solution.py:27
  77.4 2.4 %collective-permute-start.9 = (f32[4,128]{1,0:T(4,128)S(1)}, f32[4,128]{1,0:T(4,128)S(1)}, u32[]{:S(2)}, u32[]{:S(2)}) collective-permute-start(f32[4,128]{1,0:T(4,128)S(1)} %get-tuple-element.65), channel_id=1, source_target_pairs={{2,0},{4,2},{6,4},{8,6},{10,8},{12,10},{14,12},{16,14},{18,16},{20... | collective-permute-start | bytes 6152 | tf_op jit(solution)/shard_map/ppermute | solution.py:27
  79.8 3.2 %collective-permute-start.8 = (f32[4,128]{1,0:T(4,128)S(1)}, f32[4,128]{1,0:T(4,128)S(1)}, u32[]{:S(2)}, u32[]{:S(2)}) collective-permute-start(f32[4,128]{1,0:T(4,128)S(1)} %get-tuple-element.64), channel_id=1, source_target_pairs={{0,2},{2,4},{4,6},{6,8},{8,10},{10,12},{12,14},{14,16},{16,18},{18... | collective-permute-start | bytes 6152 | tf_op jit(solution)/shard_map/ppermute | solution.py:27
  83.0 26.6 %all-reduce.3.cloned.1.call-done = f32[3,4,128,256]{3,2,1,0:T(8,128)} async-done(((f32[3,4,128,256]{3,2,1,0:T(8,128)}), f32[3,4,128,256]{3,2,1,0:T(8,128)}) %all-reduce.3.cloned.1.call-update) | async-done | bytes 1572880 | tf_op jit(solution)/shard_map/psum | solution.py:123
  109.6 1.5 %slice_bitcast_fusion.2 = (f32[4,128,256]{2,1,0:T(8,128)S(1)}, f32[4,128,256]{2,1,0:T(8,128)S(1)}, f32[4,128,256]{2,1,0:T(8,128)S(1)}) fusion(f32[3,4,128,256]{3,2,1,0:T(8,128)} %all-reduce.3.cloned.1.call-done), kind=kLoop, calls=%fused_computation.51 | loop fusion | bytes 3145728 | tf_op jit(solution)/shard_map/squeeze | solution.py:124
  111.1 2.6 %collective-permute-start.5 = (f32[4,128,256]{2,1,0:T(8,128)S(1)}, f32[4,128,256]{2,1,0:T(8,128)S(1)}, u32[]{:S(2)}, u32[]{:S(2)}) collective-permute-start(f32[4,128,256]{2,1,0:T(8,128)S(1)} %get-tuple-element.62), channel_id=1, source_target_pairs={{2,0},{4,2},{6,4},{8,6},{10,8},{12,10},{14,12},{16,14},{18,16},{20... | collective-permute-start | bytes 1572872 | tf_op jit(solution)/shard_map/ppermute | solution.py:27
  113.7 3.0 %collective-permute-start.4 = (f32[4,128,256]{2,1,0:T(8,128)S(1)}, f32[4,128,256]{2,1,0:T(8,128)S(1)}, u32[]{:S(2)}, u32[]{:S(2)}) collective-permute-start(f32[4,128,256]{2,1,0:T(8,128)S(1)} %get-tuple-element.63), channel_id=1, source_target_pairs={{0,2},{2,4},{4,6},{6,8},{8,10},{10,12},{12,14},{14,16},{16,18},{18... | collective-permute-start | bytes 1572872 | tf_op jit(solution)/shard_map/ppermute | solution.py:27
  116.8 0.6 fusion.175
  117.3 0.6 fusion.173
  117.9 3.7 %collective-permute-done.5 = f32[4,128,256]{2,1,0:T(8,128)S(1)} collective-permute-done((f32[4,128,256]{2,1,0:T(8,128)S(1)}, f32[4,128,256]{2,1,0:T(8,128)S(1)}, u32[]{:S(2)}, u32[]{:S(2)}) %collective-permute-start.5) | collective-permute-done | bytes 524320 | tf_op jit(solution)/shard_map/ppermute | solution.py:27
  121.6 5.8 %collective-permute-done.4 = f32[4,128,256]{2,1,0:T(8,128)S(1)} collective-permute-done((f32[4,128,256]{2,1,0:T(8,128)S(1)}, f32[4,128,256]{2,1,0:T(8,128)S(1)}, u32[]{:S(2)}, u32[]{:S(2)}) %collective-permute-start.4) | collective-permute-done | bytes 524320 | tf_op jit(solution)/shard_map/ppermute | solution.py:27
  127.4 0.8 fusion.23
  (62 shorter events, 3.6 us)
Async XLA Ops:
  7.2 31.3 %copy-start = (bf16[128,256]{1,0:T(8,128)(2,1)S(1)}, bf16[128,256]{1,0:T(8,128)(2,1)}, u32[]{:S(2)}) copy-start(bf16[128,256]{1,0:T(8,128)(2,1)} %param.7) | copy-start | bytes 196612
  7.2 45.3 %copy-start.2 = (bf16[512,256]{1,0:T(8,128)(2,1)S(1)}, bf16[512,256]{1,0:T(8,128)(2,1)}, u32[]{:S(2)}) copy-start(bf16[512,256]{1,0:T(8,128)(2,1)} %param.10) | copy-start | bytes 786436
  7.2 45.2 %collective-permute-start.2 = (bf16[512,256]{1,0:T(8,128)(2,1)}, bf16[512,256]{1,0:T(8,128)(2,1)S(1)}, u32[]{:S(2)}, u32[]{:S(2)}) collective-permute-start(bf16[512,256]{1,0:T(8,128)(2,1)} %param.10), channel_id=1, source_target_pairs={{0,2},{2,4},{4,6},{6,8},{8,10},{10,12},{12,14},{14,16},{16,18},{18... | collective-permute-start | bytes 786440 | tf_op jit(solution)/shard_map/ppermute | solution.py:16
  11.9 40.6 %collective-permute-start.3 = (bf16[512,256]{1,0:T(8,128)(2,1)}, bf16[512,256]{1,0:T(8,128)(2,1)S(1)}, u32[]{:S(2)}, u32[]{:S(2)}) collective-permute-start(bf16[512,256]{1,0:T(8,128)(2,1)} %param.10), channel_id=1, source_target_pairs={{2,0},{4,2},{6,4},{8,6},{10,8},{12,10},{14,12},{16,14},{18,16},{20... | collective-permute-start | bytes 786440 | tf_op jit(solution)/shard_map/ppermute | solution.py:19
  15.2 31.2 %collective-permute-start.1 = (bf16[512,2]{0,1:T(2,128)(2,1)S(1)}, bf16[512,2]{0,1:T(2,128)(2,1)S(1)}, u32[]{:S(2)}, u32[]{:S(2)}) collective-permute-start(bf16[512,2]{0,1:T(2,128)(2,1)S(1)} %pad_maximum_fusion.1), channel_id=1, source_target_pairs={{2,0},{4,2},{6,4},{8,6},{10,8},{12,10},{14,12},{16,14},{18,16},{20... | collective-permute-start | bytes 6152 | tf_op jit(solution)/shard_map/ppermute | solution.py:19
  17.1 29.3 %collective-permute-start = (bf16[512,2]{0,1:T(2,128)(2,1)S(1)}, bf16[512,2]{0,1:T(2,128)(2,1)S(1)}, u32[]{:S(2)}, u32[]{:S(2)}) collective-permute-start(bf16[512,2]{0,1:T(2,128)(2,1)S(1)} %pad_maximum_fusion.1), channel_id=1, source_target_pairs={{0,2},{2,4},{4,6},{6,8},{8,10},{10,12},{12,14},{14,16},{16,18},{18... | collective-permute-start | bytes 6152 | tf_op jit(solution)/shard_map/ppermute | solution.py:16
  26.3 13.9 %all-to-all-start.1 = ((bf16[16,1,8]{2,1,0:T(2,128)(2,1)}), bf16[16,1,8]{2,1,0:T(2,128)(2,1)S(1)}, u32[]{:S(2)}, u32[]{:S(2)}) async-start(bf16[16,1,8]{2,1,0:T(2,128)(2,1)} %select_n.63), calls=%async_computation.1 | async-start | bytes 16384 | tf_op jit(solution)/shard_map/all_to_all | solution.py:65
  40.2 12.1 %all-to-all-start = ((bf16[16,8,256]{2,1,0:T(8,128)(2,1)}), bf16[16,8,256]{2,1,0:T(8,128)(2,1)S(1)}, u32[]{:S(2)}, u32[]{:S(2)}) async-start(bf16[16,8,256]{2,1,0:T(8,128)(2,1)} %bitcast_select_fusion), calls=%async_computation | async-start | bytes 131072 | tf_op jit(solution)/shard_map/all_to_all | solution.py:64
  46.2 63.4 %all-reduce.3.cloned.1.call-start = ((), (), s32[]{:S(2)}) async-start(), calls=%async_computation.2 | async-start | bytes 3145728 | tf_op jit(solution)/shard_map/psum | solution.py:123
  58.8 1.2 copy-start.1
  71.4 42.3 %collective-permute-start.7 = (f32[4,128]{1,0:T(4,128)S(1)}, f32[4,128]{1,0:T(4,128)S(1)}, u32[]{:S(2)}, u32[]{:S(2)}) collective-permute-start(f32[4,128]{1,0:T(4,128)S(1)} %get-tuple-element.67), channel_id=1, source_target_pairs={{2,0},{4,2},{6,4},{8,6},{10,8},{12,10},{14,12},{16,14},{18,16},{20... | collective-permute-start | bytes 6152 | tf_op jit(solution)/shard_map/ppermute | solution.py:27
  75.5 41.2 %collective-permute-start.6 = (f32[4,128]{1,0:T(4,128)S(1)}, f32[4,128]{1,0:T(4,128)S(1)}, u32[]{:S(2)}, u32[]{:S(2)}) collective-permute-start(f32[4,128]{1,0:T(4,128)S(1)} %get-tuple-element.66), channel_id=1, source_target_pairs={{0,2},{2,4},{4,6},{6,8},{8,10},{10,12},{12,14},{14,16},{16,18},{18... | collective-permute-start | bytes 6152 | tf_op jit(solution)/shard_map/ppermute | solution.py:27
  77.4 39.9 %collective-permute-start.9 = (f32[4,128]{1,0:T(4,128)S(1)}, f32[4,128]{1,0:T(4,128)S(1)}, u32[]{:S(2)}, u32[]{:S(2)}) collective-permute-start(f32[4,128]{1,0:T(4,128)S(1)} %get-tuple-element.65), channel_id=1, source_target_pairs={{2,0},{4,2},{6,4},{8,6},{10,8},{12,10},{14,12},{16,14},{18,16},{20... | collective-permute-start | bytes 6152 | tf_op jit(solution)/shard_map/ppermute | solution.py:27
  79.8 37.5 %collective-permute-start.8 = (f32[4,128]{1,0:T(4,128)S(1)}, f32[4,128]{1,0:T(4,128)S(1)}, u32[]{:S(2)}, u32[]{:S(2)}) collective-permute-start(f32[4,128]{1,0:T(4,128)S(1)} %get-tuple-element.64), channel_id=1, source_target_pairs={{0,2},{2,4},{4,6},{6,8},{8,10},{10,12},{12,14},{14,16},{16,18},{18... | collective-permute-start | bytes 6152 | tf_op jit(solution)/shard_map/ppermute | solution.py:27
  111.1 10.5 %collective-permute-start.5 = (f32[4,128,256]{2,1,0:T(8,128)S(1)}, f32[4,128,256]{2,1,0:T(8,128)S(1)}, u32[]{:S(2)}, u32[]{:S(2)}) collective-permute-start(f32[4,128,256]{2,1,0:T(8,128)S(1)} %get-tuple-element.62), channel_id=1, source_target_pairs={{2,0},{4,2},{6,4},{8,6},{10,8},{12,10},{14,12},{16,14},{18,16},{20... | collective-permute-start | bytes 1572872 | tf_op jit(solution)/shard_map/ppermute | solution.py:27
  113.7 13.7 %collective-permute-start.4 = (f32[4,128,256]{2,1,0:T(8,128)S(1)}, f32[4,128,256]{2,1,0:T(8,128)S(1)}, u32[]{:S(2)}, u32[]{:S(2)}) collective-permute-start(f32[4,128,256]{2,1,0:T(8,128)S(1)} %get-tuple-element.63), channel_id=1, source_target_pairs={{0,2},{2,4},{4,6},{6,8},{8,10},{10,12},{12,14},{14,16},{16,18},{18... | collective-permute-start | bytes 1572872 | tf_op jit(solution)/shard_map/ppermute | solution.py:27
Sparse Core Ops, SparseCore 0:
  60.1 49.4 all-reduce.2
where the time goes:
time: 136 us; the launch traced here: 135 us
  waiting for transfers between devices  41.9 us (31%)
  starting transfers between devices  41.2 us (30%)
  between operations  19.5 us (14%)
  local copies, waits for them, and re-layouts  10.1 us (7%)
  other arithmetic  8.72 us (6%)
  blocking collectives  7.14 us (5%)
  matrix products  6.53 us (5%)
    psum x1, waiting for transfers between devices, shards(): summed = lax.psum((shaped[0], shaped[1], shaped[2]), 'grp')  26.6 us
    ppermute x6, starting transfers between devices, passed_along(): return lax.ppermute(shard, axis, pairs)  17.2 us
    ppermute x6, waiting for transfers between devices, passed_along(): return lax.ppermute(shard, axis, pairs)  9.52 us
    ppermute x2, starting transfers between devices, extended(): lax.ppermute(lax.slice_in_dim(block, block.shape[dim] - width, None, axis...  8.31 us
    psum x1, blocking collectives, shards(): summed = lax.psum((shaped[0], shaped[1], shaped[2]), 'grp')  7.14 us
    all_to_all x1, starting transfers between devices, shards(): lax.all_to_all(grouped, 'tile', split_axis=0, concat_axis=0, tiled=True)  6.02 us
    all_to_all x1, starting transfers between devices, shards(): lax.all_to_all(goals, 'tile', split_axis=0, concat_axis=0, tiled=True)  5.85 us
    all_to_all x1, waiting for transfers between devices, shards(): lax.all_to_all(grouped, 'tile', split_axis=0, concat_axis=0, tiled=True)  5.73 us
  transfers between devices with their start and end apart: 13, of which 4 were waited for; matrix products, arithmetic and copies ran while one was open for 13% of the time, Pallas kernels for 0%

commit v1 on v0

v1 whole, which is shorter than its diff:
```python
import functools
import math

import jax
import jax.numpy as jnp
from jax import lax
from jax.experimental import pallas as pl
from jax.experimental.pallas import tpu as pltpu
from jax.sharding import PartitionSpec as P

BS = 128
LANES = 128
F32 = jnp.float32
BF16 = jnp.bfloat16
MESH = pl.DeviceIdType.MESH
NT = (((1,), (1,)), ((), ()))


def iota(shape, dim):
    return lax.broadcasted_iota(jnp.int32, shape, dim)


def repeat(count, body):
    if count <= 16:
        for index in range(count):
            body(index)
    else:
        lax.fori_loop(0, count, lambda index, carry: (body(index), carry)[1], 0)


def to_column(row):
    eye = iota((LANES, LANES), 0) == iota((LANES, LANES), 1)
    return jnp.sum(jnp.where(eye, row, 0.0), axis=1, keepdims=True)


def to_row(column):
    eye = iota((LANES, LANES), 0) == iota((LANES, LANES), 1)
    return jnp.sum(jnp.where(eye, column, 0.0), axis=0, keepdims=True)


def kernel(
    tiles, groups,
    points, targets, morton, inducing, means, scales, neighbours,
    grad_rows, grad_means, grad_scales,
    grouped, landed, feats, mine_part, parts, dist, value, slope, errors,
    send1, recv1, send2, recv2, send3, recv3,
):
    rows, width = points.shape
    per = rows // tiles
    owned = means.shape[0]
    mine = owned // groups
    size = mine * BS
    count = neighbours.shape[1]
    chunks = rows // LANES
    here = lax.axis_index("tile")
    grp = lax.axis_index("grp")

    def exists(tile):
        return (tile >= 0) & (tile < tiles)

    def other(step):
        return lax.rem(grp + step, groups)

    def source(step):
        return lax.rem(grp + groups - step, groups)

    barrier = pltpu.get_barrier_semaphore()

    def greet(step):
        pl.semaphore_signal(
            barrier, inc=1,
            device_id=(lax.rem(here + step + 1, tiles), grp), device_id_type=MESH,
        )

    repeat(tiles - 1, greet)
    expected = jnp.int32(tiles - 1)
    for d in range(-2, 3):
        there = exists(here + d)
        expected += jnp.where(there, groups - 1, 0)

        @pl.when(there)
        def _():
            for step in range(1, groups):
                pl.semaphore_signal(
                    barrier, inc=1, device_id=(here + d, other(step)), device_id_type=MESH
                )

        if d:
            @pl.when(jnp.logical_not(there))
            def _():
                parts[d + 2] = jnp.zeros(parts.shape[1:], F32)
                if abs(d) == 1:
                    feats[d + 1] = jnp.zeros(feats.shape[1:], BF16)

    codes = morton[...]
    member = iota((tiles, rows), 0) == codes
    before = jnp.dot(
        member.astype(F32).astype(BF16),
        (iota((rows, rows), 0) < iota((rows, rows), 1)).astype(F32).astype(BF16),
        preferred_element_type=F32,
    )
    rank = jnp.sum(jnp.where(member, before, 0.0), axis=0, keepdims=True)
    place = codes * per + rank.astype(jnp.int32)
    chosen = iota((rows, rows), 0) == place
    moved = jnp.dot(
        chosen.astype(F32).astype(BF16), points[...], preferred_element_type=F32
    )
    goals = jnp.sum(jnp.where(chosen, targets[...].astype(F32), 0.0), axis=1, keepdims=True)
    grouped[:, :, :width] = moved.reshape(tiles, per, width).astype(BF16)
    grouped[:, :, width:] = (
        jnp.broadcast_to(goals, (rows, LANES)).reshape(tiles, per, LANES).astype(BF16)
    )
    pl.semaphore_wait(barrier, expected)

    def first(step):
        to = lax.rem(here + step + 1, tiles)
        return pltpu.make_async_remote_copy(
            src_ref=grouped.at[to], dst_ref=landed.at[here],
            send_sem=send1.at[step], recv_sem=recv1.at[step],
            device_id=(to, grp), device_id_type=MESH,
        )

    repeat(tiles - 1, lambda step: first(step).start())
    landed[here] = grouped[here]

    own = inducing[pl.ds(pl.multiple_of(grp * size, size), size), :]
    own_f = own.astype(F32)
    own_sq = jnp.sum(own_f * own_f, axis=1, keepdims=True)

    def own_column(ref):
        every = ref[...].astype(F32)
        picked = [
            to_column(jnp.sum(
                jnp.where(iota(every.shape, 0) == grp * mine + b, every, 0.0),
                axis=0, keepdims=True,
            ))
            for b in range(mine)
        ]
        return jnp.concatenate(picked, axis=0)

    mean = own_column(means)
    scale = own_column(scales)
    scaled = scale / (2.0 * width)
    times = []
    for r in range(3):
        tile = here + r - 1
        row = jnp.clip(tile, 0, tiles - 1)
        pieces = []
        for b in range(mine):
            block = here * owned + grp * mine + b
            listed = jnp.int32(0)
            for k in range(count):
                listed += jnp.where(neighbours[row, k] == block, 1, 0)
            listed = jnp.where(exists(tile), listed, 0)
            pieces.append(jnp.full((BS, 1), listed.astype(F32), F32))
        times.append(jnp.concatenate(pieces, axis=0))

    repeat(tiles - 1, lambda step: first(step).wait_recv())
    arrived = landed[...].astype(F32).reshape(rows, width + LANES)
    feats[1, grp] = arrived[:, :width].astype(BF16)

    def second(d, step):
        return pltpu.make_async_remote_copy(
            src_ref=feats.at[1, grp], dst_ref=feats.at[1 - d, grp],
            send_sem=send2.at[1 - d, step], recv_sem=recv2.at[1 - d, step],
            device_id=(here + d, other(step)), device_id_type=MESH,
        )

    hops = [(d, s) for d in (1, -1, 0) for s in range(groups) if (d, s) != (0, 0)]
    for d, s in hops:
        @pl.when(exists(here + d))
        def _():
            second(d, s).start()

    ones = jnp.ones((8, width), BF16)

    def forward(r, group):
        def piece(c):
            span = pl.ds(pl.multiple_of(c * LANES, LANES), LANES)
            block = feats[r, group, span, :]
            block_f = block.astype(F32)
            square = block_f * block_f
            high = square.astype(BF16)
            low = (square - high.astype(F32)).astype(BF16)
            feat_sq = (
                lax.dot_general(ones, high, NT, preferred_element_type=F32)
                + lax.dot_general(ones, low, NT, preferred_element_type=F32)
            )[:1]
            cross = lax.dot_general(own, block, NT, preferred_element_type=F32)
            far = (feat_sq + own_sq) - 2.0 * cross
            radius = jnp.sqrt(jnp.maximum(scaled * far, 0.0))
            remain = 1.0 - jnp.minimum(radius, 1.0)
            square_r = remain * remain
            height = square_r * square_r * (4.0 * radius + 1.0)
            dist[r, group, :, span] = far
            value[r, group, :, span] = height
            slope[r, group, :, span] = -10.0 * (square_r * remain)
            mine_part[r, group, :, span] = jnp.sum(
                (mean * times[r]) * height, axis=0, keepdims=True
            )

        repeat(chunks, piece)

    forward(1, grp)
    for c in range(chunks):
        span = pl.ds(c * LANES, LANES)
        goal = to_row(arrived[c * LANES:(c + 1) * LANES, width:])
        mine_part[1, grp, :, span] = mine_part[1, grp, :, span] - goal

    order = [(r, s) for r in (1, 0, 2) for s in range(groups) if (r, s) != (1, 0)]
    for r, s in order:
        @pl.when(exists(here + r - 1))
        def _():
            second(1 - r, s).wait_recv()

        forward(r, source(s))

    def third(d, step):
        return pltpu.make_async_remote_copy(
            src_ref=mine_part, dst_ref=parts.at[2 - d, grp],
            send_sem=send3.at[2 - d, step], recv_sem=recv3.at[2 - d, step],
            device_id=(here + d, other(step)), device_id_type=MESH,
        )

    spread = [(d, s) for d in range(-2, 3) for s in range(groups) if (d, s) != (0, 0)]
    for d, s in spread:
        @pl.when(exists(here + d))
        def _():
            third(d, s).start()

    parts[2, grp] = mine_part[...]
    for d, s in spread:
        @pl.when(exists(here - d))
        def _():
            third(d, s).wait_recv()

    total_mean = jnp.zeros((size, 1), F32)
    total_scale = jnp.zeros((size, 1), F32)
    total_column = jnp.zeros((size, 1), F32)
    total_back = jnp.zeros((size, width), F32)
    for r in range(3):
        for group in range(groups):
            error = jnp.zeros((1, rows), F32)
            for d in range(r - 2, r + 1):
                for sender in range(groups):
                    error = error + parts[d + 2, sender, r - d, group]
            errors[group] = error

        def backward(index, carry):
            sum_mean, sum_scale, sum_column, back = carry
            group, c = index // chunks, lax.rem(index, chunks)
            span = pl.ds(pl.multiple_of(c * LANES, LANES), LANES)
            error = errors[group, :, span]
            weight = (error * mean) * slope[r, group, :, span]
            sum_mean = sum_mean + error * value[r, group, :, span]
            sum_scale = sum_scale + weight * dist[r, group, :, span]
            sum_column = sum_column + weight
            back = back + jnp.dot(
                weight.astype(BF16), feats[r, group, span, :], preferred_element_type=F32
            )
            return sum_mean, sum_scale, sum_column, back

        flat = jnp.zeros((size, LANES), F32)
        carry = (flat, flat, flat, jnp.zeros((size, width), F32))
        if groups * chunks <= 4:
            for index in range(groups * chunks):
                carry = backward(jnp.int32(index), carry)
        else:
            carry = lax.fori_loop(0, groups * chunks, backward, carry)
        total_mean += times[r] * jnp.sum(carry[0], axis=1, keepdims=True)
        total_scale += times[r] * jnp.sum(carry[1], axis=1, keepdims=True)
        total_column += times[r] * jnp.sum(carry[2], axis=1, keepdims=True)
        total_back += times[r] * carry[3]

    norm = 1.0 / math.sqrt(rows * groups)
    grad_rows[...] = (scale * (norm / width)) * (own_f * total_column - total_back)
    for b in range(mine):
        at = slice(b * BS, (b + 1) * BS)
        grad_means[:, at] = to_row(total_mean[at]) * norm
        grad_scales[:, at] = to_row(total_scale[at]) * (norm / (2.0 * width))

    repeat(tiles - 1, lambda step: first(step).wait_send())
    for d, s in hops:
        @pl.when(exists(here + d))
        def _():
            second(d, s).wait_send()
    for d, s in spread:
        @pl.when(exists(here + d))
        def _():
            third(d, s).wait_send()


def shards(points, targets, morton, inducing, means, scales, neighbours):
    tiles = lax.axis_size("tile")
    groups = lax.axis_size("grp")
    rows, width = points.shape
    per = rows // tiles
    owned = inducing.shape[0] // BS
    size = owned // groups * BS
    vmem = pl.BlockSpec(memory_space=pltpu.VMEM)
    dma = pltpu.SemaphoreType.DMA
    pair = (3, groups, size, rows)
    result = pl.pallas_call(
        functools.partial(kernel, tiles, groups),
        out_shape=(
            jax.ShapeDtypeStruct((size, width), F32),
            jax.ShapeDtypeStruct((1, size), F32),
            jax.ShapeDtypeStruct((1, size), F32),
        ),
        in_specs=[vmem] * 6 + [pl.BlockSpec(memory_space=pltpu.SMEM)],
        out_specs=(vmem, vmem, vmem),
        scratch_shapes=[
            pltpu.VMEM((tiles, per, width + LANES), BF16),
            pltpu.VMEM((tiles, per, width + LANES), BF16),
            pltpu.VMEM((3, groups, rows, width), BF16),
            pltpu.VMEM((3, groups, 1, rows), F32),
            pltpu.VMEM((5, groups, 3, groups, 1, rows), F32),
            pltpu.VMEM(pair, F32),
            pltpu.VMEM(pair, F32),
            pltpu.VMEM(pair, F32),
            pltpu.VMEM((groups, 1, rows), F32),
            dma((tiles - 1,)), dma((tiles - 1,)),
            dma((3, groups)), dma((3, groups)),
            dma((5, groups)), dma((5, groups)),
        ],
        compiler_params=pltpu.CompilerParams(
            collective_id=0, has_side_effects=True, vmem_limit_bytes=48 << 20
        ),
    )(
        points, targets.reshape(1, rows), morton.reshape(1, rows), inducing,
        means.reshape(owned, BS), scales.reshape(owned, BS), neighbours,
    )
    return result[0], result[1].reshape(size), result[2].reshape(size)


def solution(mesh):
    placed = (
        P(("tile", "grp"), None),
        P(("tile", "grp")),
        P(("tile", "grp")),
        P("tile", None),
        P("tile"),
        P("tile"),
        P(),
    )
    return jax.shard_map(
        shards,
        mesh=mesh,
        in_specs=placed,
        out_specs=(P(("tile", "grp"), None), P(("tile", "grp")), P(("tile", "grp"))),
        check_vma=False,
    )
```

time: 136 us -> 27.9 us (0.21)
  the two profiles are of different devices: /device:TPU:1 before, /device:TPU:0 now
where the time goes in v1:
time: 27.9 us; the launch traced here: 27.7 us
  Pallas kernels  22 us (79%)
  local copies, waits for them, and re-layouts  4.99 us (18%)
  between operations  0.66 us (2%)
    pallas_call x1, Pallas kernels, shards(): pl.pallas_call(functools.partial(kernel, tiles, groups), out_shape=(jax.S...  22 us
    unnamed x18, local copies, waits for them, and re-layouts  4.99 us

profile of v1, /device:TPU:0, one launch (start us, length us, event | category | flops | bytes accessed | tf_op | source)
XLA Modules:
  0.0 27.7 jit_solution(17140632241274919238)
XLA Ops:
  0.6 0.0 copy-start.6
  0.6 0.7 %copy-done.6 = s32[16,8]{0,1:T(8,128)S(1)} copy-done((s32[16,8]{0,1:T(8,128)S(1)}, s32[16,8]{0,1:T(8,128)}, u32[]{:S(2)}) %copy-start.6) | copy-done | bytes 536
  1.3 0.0 copy-start.2
  1.3 0.0 copy-start.3
  1.3 0.0 copy-start.4
  1.3 0.0 copy-start.5
  1.3 0.1 copy.10.neighbours
  1.4 0.6 %copy-done.2 = bf16[512]{0:T(512)(128)(2,1)S(1)} copy-done((bf16[512]{0:T(512)(128)(2,1)S(1)}, bf16[512]{0:T(512)(128)(2,1)}, u32[]{:S(2)}) %copy-start.2) | copy-done | bytes 1048
  2.0 0.0 copy-done.3
  2.0 0.0 copy-done.4
  2.0 0.0 copy-done.5
  2.0 0.0 copy-start
  2.0 0.9 %copy-done = bf16[512,256]{1,0:T(8,128)(2,1)S(1)} copy-done((bf16[512,256]{1,0:T(8,128)(2,1)S(1)}, bf16[512,256]{1,0:T(8,128)(2,1)}, u32[]{:S(2)}) %copy-start) | copy-done | bytes 262168
  3.0 0.0 copy-start.1
  3.0 0.8 %copy-done.1 = bf16[128,256]{1,0:T(8,128)(2,1)S(1)} copy-done((bf16[128,256]{1,0:T(8,128)(2,1)S(1)}, bf16[128,256]{1,0:T(8,128)(2,1)}, u32[]{:S(2)}) %copy-start.1) | copy-done | bytes 65560
  3.8 22.0 %shard_map.94 = (f32[256,256]{1,0:T(8,128)S(1)}, f32[1,256]{1,0:T(1,128)S(1)}, f32[1,256]{1,0:T(1,128)S(1)}) custom-call(bf16[128,256]{1,0:T(8,128)(2,1)S(1)} %copy-done.1, bf16[1,128]{1,0:T(2,128)(2,1)S(1)} %bitcast.10, s32[1,128]{1,0:T(1,128)S(1)} %bitcast.11, bf16[512,256]{1,0:T(8,128)(2,1)S(1)} %copy-done, bf16[4,128]{1,0:T(4,128)(2,1)S(1)} %bitcast.6, ...), custom_call_target="tpu_custom_call" | custom-call | tf_op jit(solution)/shard_map/pallas_call | solution.py:303
  25.9 0.7 %copy.14 = f32[256,256]{1,0:T(8,128)} copy(f32[256,256]{1,0:T(8,128)S(1)} %get-tuple-element.12) | data formatting | bytes 524288
  26.6 0.6 %copy.15 = f32[256]{0:T(256)} copy(f32[256]{0:T(256)S(1)} %bitcast.9) | data formatting | bytes 2048
  27.1 0.6 %copy.16 = f32[256]{0:T(256)} copy(f32[256]{0:T(256)S(1)} %bitcast.8) | data formatting | bytes 2048
Async XLA Ops:
  0.6 0.7 %copy-start.6 = (s32[16,8]{0,1:T(8,128)S(1)}, s32[16,8]{0,1:T(8,128)}, u32[]{:S(2)}) copy-start(s32[16,8]{0,1:T(8,128)} %param.13) | copy-start | bytes 1540
  1.3 0.7 %copy-start.2 = (bf16[512]{0:T(512)(128)(2,1)S(1)}, bf16[512]{0:T(512)(128)(2,1)}, u32[]{:S(2)}) copy-start(bf16[512]{0:T(512)(128)(2,1)} %param.11) | copy-start | bytes 3076
  1.3 0.7 %copy-start.3 = (bf16[512]{0:T(512)(128)(2,1)S(1)}, bf16[512]{0:T(512)(128)(2,1)}, u32[]{:S(2)}) copy-start(bf16[512]{0:T(512)(128)(2,1)} %param.12) | copy-start | bytes 3076
  1.3 0.7 %copy-start.4 = (bf16[128]{0:T(256)(128)(2,1)S(1)}, bf16[128]{0:T(256)(128)(2,1)}, u32[]{:S(2)}) copy-start(bf16[128]{0:T(256)(128)(2,1)} %param.8) | copy-start | bytes 772
  1.3 0.7 %copy-start.5 = (s32[128]{0:T(128)S(1)}, s32[128]{0:T(128)}, u32[]{:S(2)}) copy-start(s32[128]{0:T(128)} %param.9) | copy-start | bytes 1540
  2.0 0.9 %copy-start = (bf16[512,256]{1,0:T(8,128)(2,1)S(1)}, bf16[512,256]{1,0:T(8,128)(2,1)}, u32[]{:S(2)}) copy-start(bf16[512,256]{1,0:T(8,128)(2,1)} %inducing.1) | copy-start | bytes 786436
  3.0 0.8 %copy-start.1 = (bf16[128,256]{1,0:T(8,128)(2,1)S(1)}, bf16[128,256]{1,0:T(8,128)(2,1)}, u32[]{:S(2)}) copy-start(bf16[128,256]{1,0:T(8,128)(2,1)} %points.1) | copy-start | bytes 196612

commit v2 on v1

--- a/solution.py
+++ b/solution.py
@@ -40,8 +40,9 @@
 
 def kernel(
     tiles, groups,
-    points, targets, morton, inducing, means, scales, neighbours,
+    points_in, targets_in, morton_in, inducing_in, means_in, scales_in, neighbours_in,
     grad_rows, grad_means, grad_scales,
+    points, targets, morton, inducing, means, scales, neighbours, loads,
     grouped, landed, feats, mine_part, parts, dist, value, slope, errors,
     send1, recv1, send2, recv2, send3, recv3,
 ):
@@ -50,10 +51,23 @@
     owned = means.shape[0]
     mine = owned // groups
     size = mine * BS
-    count = neighbours.shape[1]
+    count = neighbours.shape[0]
     chunks = rows // LANES
     here = lax.axis_index("tile")
     grp = lax.axis_index("grp")
+
+    own_rows = pl.ds(pl.multiple_of(grp * size, size), size)
+    pairs = (
+        (morton_in, morton), (points_in, points), (targets_in, targets),
+        (inducing_in.at[own_rows, :], inducing), (means_in, means),
+        (scales_in, scales), (neighbours_in, neighbours),
+    )
+    load = [
+        pltpu.make_async_copy(pair[0], pair[1], loads.at[index])
+        for index, pair in enumerate(pairs)
+    ]
+    for copy in load[:2]:
+        copy.start()
 
     def exists(tile):
         return (tile >= 0) & (tile < tiles)
@@ -73,6 +87,8 @@
         )
 
     repeat(tiles - 1, greet)
+    for copy in load[2:]:
+        copy.start()
     expected = jnp.int32(tiles - 1)
     for d in range(-2, 3):
         there = exists(here + d)
@@ -91,6 +107,9 @@
                 parts[d + 2] = jnp.zeros(parts.shape[1:], F32)
                 if abs(d) == 1:
                     feats[d + 1] = jnp.zeros(feats.shape[1:], BF16)
+
+    for copy in load[:3]:
+        copy.wait()
 
     codes = morton[...]
     member = iota((tiles, rows), 0) == codes
@@ -123,7 +142,9 @@
     repeat(tiles - 1, lambda step: first(step).start())
     landed[here] = grouped[here]
 
-    own = inducing[pl.ds(pl.multiple_of(grp * size, size), size), :]
+    for copy in load[3:]:
+        copy.wait()
+    own = inducing[...]
     own_f = own.astype(F32)
     own_sq = jnp.sum(own_f * own_f, axis=1, keepdims=True)
 
@@ -150,7 +171,7 @@
             block = here * owned + grp * mine + b
             listed = jnp.int32(0)
             for k in range(count):
-                listed += jnp.where(neighbours[row, k] == block, 1, 0)
+                listed += jnp.where(neighbours[k, row] == block, 1, 0)
             listed = jnp.where(exists(tile), listed, 0)
             pieces.append(jnp.full((BS, 1), listed.astype(F32), F32))
         times.append(jnp.concatenate(pieces, axis=0))
@@ -159,22 +180,39 @@
     arrived = landed[...].astype(F32).reshape(rows, width + LANES)
     feats[1, grp] = arrived[:, :width].astype(BF16)
 
-    def second(d, step):
+    near = 1 - 2 * lax.rem(here, 2)
+
+    def share(d, step, group, to):
         return pltpu.make_async_remote_copy(
-            src_ref=feats.at[1, grp], dst_ref=feats.at[1 - d, grp],
+            src_ref=feats.at[1, group], dst_ref=feats.at[1 - d, group],
             send_sem=send2.at[1 - d, step], recv_sem=recv2.at[1 - d, step],
-            device_id=(here + d, other(step)), device_id_type=MESH,
+            device_id=(here + d, to), device_id_type=MESH,
         )
 
-    hops = [(d, s) for d in (1, -1, 0) for s in range(groups) if (d, s) != (0, 0)]
-    for d, s in hops:
-        @pl.when(exists(here + d))
-        def _():
-            second(d, s).start()
+    def across(step):
+        return share(0, step, grp, other(step))
+
+    def far_copy(step):
+        return share(-near, step, grp, other(step))
+
+    def near_copy(step):
+        return share(near, step, source(step), grp)
+
+    for s in range(1, groups):
+        across(s).start()
+
+    @pl.when(exists(here + near))
+    def _():
+        near_copy(0).start()
+
+    @pl.when(exists(here - near))
+    def _():
+        for s in range(groups):
+            far_copy(s).start()
 
     ones = jnp.ones((8, width), BF16)
 
-    def forward(r, group):
+    def forward(r, group, listed):
         def piece(c):
             span = pl.ds(pl.multiple_of(c * LANES, LANES), LANES)
             block = feats[r, group, span, :]
@@ -196,24 +234,34 @@
             value[r, group, :, span] = height
             slope[r, group, :, span] = -10.0 * (square_r * remain)
             mine_part[r, group, :, span] = jnp.sum(
-                (mean * times[r]) * height, axis=0, keepdims=True
+                (mean * listed) * height, axis=0, keepdims=True
             )
 
         repeat(chunks, piece)
 
-    forward(1, grp)
+    forward(1, grp, times[1])
     for c in range(chunks):
         span = pl.ds(c * LANES, LANES)
         goal = to_row(arrived[c * LANES:(c + 1) * LANES, width:])
         mine_part[1, grp, :, span] = mine_part[1, grp, :, span] - goal
 
-    order = [(r, s) for r in (1, 0, 2) for s in range(groups) if (r, s) != (1, 0)]
-    for r, s in order:
-        @pl.when(exists(here + r - 1))
+    for s in range(1, groups):
+        across(s).wait_recv()
+
+        @pl.when(exists(here + near))
         def _():
-            second(1 - r, s).wait_recv()
-
-        forward(r, source(s))
+            near_copy(s).start()
+
+        forward(1, source(s), times[1])
+
+    for side in (near, -near):
+        listed = jnp.where(side > 0, times[2], times[0])
+        for s in range(groups):
+            @pl.when(exists(here + side))
+            def _():
+                share(-side, s, source(s), grp).wait_recv()
+
+            forward(1 + side, source(s), listed)
 
     def third(d, step):
         return pltpu.make_async_remote_copy(
@@ -280,14 +328,29 @@
         grad_scales[:, at] = to_row(total_scale[at]) * (norm / (2.0 * width))
 
     repeat(tiles - 1, lambda step: first(step).wait_send())
-    for d, s in hops:
-        @pl.when(exists(here + d))
-        def _():
-            second(d, s).wait_send()
+    for s in range(1, groups):
+        across(s).wait_send()
+
+    @pl.when(exists(here + near))
+    def _():
+        for s in range(groups):
+            near_copy(s).wait_send()
+
+    @pl.when(exists(here - near))
+    def _():
+        for s in range(groups):
+            far_copy(s).wait_send()
+
     for d, s in spread:
         @pl.when(exists(here + d))
         def _():
             third(d, s).wait_send()
+
+
+def finish(rows, means, scales, out_rows, out_means, out_scales):
+    out_rows[...] = rows[...]
+    out_means[...] = means[...]
+    out_scales[...] = scales[...]
 
 
 def shards(points, targets, morton, inducing, means, scales, neighbours):
@@ -307,9 +370,17 @@
             jax.ShapeDtypeStruct((1, size), F32),
             jax.ShapeDtypeStruct((1, size), F32),
         ),
-        in_specs=[vmem] * 6 + [pl.BlockSpec(memory_space=pltpu.SMEM)],
+        in_specs=[pl.BlockSpec(memory_space=pltpu.HBM)] * 7,
         out_specs=(vmem, vmem, vmem),
         scratch_shapes=[
+            pltpu.VMEM((rows, width), BF16),
+            pltpu.VMEM((1, rows), BF16),
+            pltpu.VMEM((1, rows), jnp.int32),
+            pltpu.VMEM((size, width), BF16),
+            pltpu.VMEM((owned, BS), BF16),
+            pltpu.VMEM((owned, BS), BF16),
+            pltpu.SMEM(neighbours.shape[::-1], jnp.int32),
+            dma((7,)),
             pltpu.VMEM((tiles, per, width + LANES), BF16),
             pltpu.VMEM((tiles, per, width + LANES), BF16),
             pltpu.VMEM((3, groups, rows, width), BF16),
@@ -324,12 +395,18 @@
             dma((5, groups)), dma((5, groups)),
         ],
         compiler_params=pltpu.CompilerParams(
-            collective_id=0, has_side_effects=True, vmem_limit_bytes=48 << 20
+            collective_id=0, has_side_effects=True, vmem_limit_bytes=62 << 20
         ),
     )(
         points, targets.reshape(1, rows), morton.reshape(1, rows), inducing,
-        means.reshape(owned, BS), scales.reshape(owned, BS), neighbours,
-    )
+        means.reshape(owned, BS), scales.reshape(owned, BS), neighbours.T,
+    )
+    result = pl.pallas_call(
+        finish,
+        out_shape=[jax.ShapeDtypeStruct(part.shape, F32) for part in result],
+        in_specs=[vmem] * 3,
+        out_specs=[vmem] * 3,
+    )(*result)
     return result[0], result[1].reshape(size), result[2].reshape(size)
 
 

time: 27.9 us -> 22.9 us (0.82)
  local copies, waits for them, and re-layouts: 4.99 us -> 0 us
    unnamed x18 -> x0, local copies, waits for them, and re-layouts: 4.99 us -> none
    pallas_call x0 -> x1, Pallas kernels: none -> 1.68 us  [shards(): pl.pallas_call(finish, out_shape=[jax.ShapeDtypeStruct(part.shape, F32) f...]
    pallas_call x1, Pallas kernels: 22 us -> 20.5 us  [shards(): pl.pallas_call(functools.partial(kernel, tiles, groups), out_shape=(jax.S...]
where the time goes in v2:
time: 22.9 us; the launch traced here: 22.8 us
  Pallas kernels  22.2 us (97%)
  between operations  0.64 us (3%)
    pallas_call x1, Pallas kernels, shards(): pl.pallas_call(functools.partial(kernel, tiles, groups), out_shape=(jax.S...  20.5 us
    pallas_call x1, Pallas kernels, shards(): pl.pallas_call(finish, out_shape=[jax.ShapeDtypeStruct(part.shape, F32) f...  1.68 us

profile of v2, /device:TPU:0, one launch (start us, length us, event | category | flops | bytes accessed | tf_op | source)
XLA Modules:
  0.0 22.8 jit_solution(13186622241319752500)
XLA Ops:
  0.6 20.5 %shard_map.94 = (f32[256,256]{1,0:T(8,128)}, f32[1,256]{1,0:T(1,128)}, f32[1,256]{1,0:T(1,128)}) custom-call(bf16[128,256]{1,0:T(8,128)(2,1)} %points_in.1, bf16[1,128]{1,0:T(2,128)(2,1)} %bitcast.10, s32[1,128]{1,0:T(1,128)} %bitcast.11, bf16[512,256]{1,0:T(8,128)(2,1)} %inducing_in.1, bf16[4,128]{1,0:T(4,128)(2,1)} %bitcast.8, bf16[4,128]{1,0:T(4,128)(2,1)} %bitcast.9, ...), custom_call_target="tpu_custom_call" | custom-call | tf_op jit(solution)/shard_map/pallas_call | solution.py:366
  21.1 1.7 %shard_map.95 = (f32[256,256]{1,0:T(8,128)}, f32[1,256]{1,0:T(1,128)}, f32[1,256]{1,0:T(1,128)}) custom-call(f32[256,256]{1,0:T(8,128)} %get-tuple-element.9.rows, f32[1,256]{1,0:T(1,128)} %get-tuple-element.10.means, f32[1,256]{1,0:T(1,128)} %get-tuple-element.11.scales), custom_call_target="tpu_custom_call" | custom-call | tf_op jit(solution)/shard_map/pallas_call | solution.py:404

commit v3 on v2

--- a/solution.py
+++ b/solution.py
@@ -176,40 +176,58 @@
             pieces.append(jnp.full((BS, 1), listed.astype(F32), F32))
         times.append(jnp.concatenate(pieces, axis=0))
 
-    repeat(tiles - 1, lambda step: first(step).wait_recv())
-    arrived = landed[...].astype(F32).reshape(rows, width + LANES)
-    feats[1, grp] = arrived[:, :width].astype(BF16)
-
     near = 1 - 2 * lax.rem(here, 2)
 
-    def share(d, step, group, to):
+    half = tiles // 2
+    front = here // half
+
+    def part(k):
+        return front if k == 0 else 1 - front
+
+    def share(d, step, group, to, k):
+        span = pl.ds(pl.multiple_of(part(k) * (rows // 2), rows // 2), rows // 2)
         return pltpu.make_async_remote_copy(
-            src_ref=feats.at[1, group], dst_ref=feats.at[1 - d, group],
-            send_sem=send2.at[1 - d, step], recv_sem=recv2.at[1 - d, step],
+            src_ref=feats.at[1, group, span, :], dst_ref=feats.at[1 - d, group, span, :],
+            send_sem=send2.at[1 - d, step, k], recv_sem=recv2.at[1 - d, step, k],
             device_id=(here + d, to), device_id_type=MESH,
         )
 
-    def across(step):
-        return share(0, step, grp, other(step))
-
-    def far_copy(step):
-        return share(-near, step, grp, other(step))
-
-    def near_copy(step):
-        return share(near, step, source(step), grp)
-
-    for s in range(1, groups):
-        across(s).start()
-
-    @pl.when(exists(here + near))
-    def _():
-        near_copy(0).start()
-
-    @pl.when(exists(here - near))
-    def _():
-        for s in range(groups):
-            far_copy(s).start()
-
+    def across(step, k):
+        return share(0, step, grp, other(step), k)
+
+    def far_copy(step, k):
+        return share(-near, step, grp, other(step), k)
+
+    def near_copy(step, k):
+        return share(near, step, source(step), grp, k)
+
+    for k in range(2):
+        def landing(index):
+            tile = part(k) * half + index
+
+            @pl.when(tile != here)
+            def _():
+                first(lax.rem(here - tile - 1 + tiles, tiles)).wait_recv()
+
+        repeat(half, landing)
+        mine_half = landed[pl.ds(part(k) * half, half), :, :].astype(F32)
+        mine_half = mine_half.reshape(rows // 2, width + LANES)
+        span = pl.ds(pl.multiple_of(part(k) * (rows // 2), rows // 2), rows // 2)
+        feats[1, grp, span, :] = mine_half[:, :width].astype(BF16)
+
+        for s in range(1, groups):
+            across(s, k).start()
+
+        @pl.when(exists(here + near))
+        def _():
+            near_copy(0, k).start()
+
+        @pl.when(exists(here - near))
+        def _():
+            for s in range(groups):
+                far_copy(s, k).start()
+
+    arrived = landed[:, :, width:].astype(F32).reshape(rows, LANES)
     ones = jnp.ones((8, width), BF16)
 
     def forward(r, group, listed):
@@ -242,15 +260,16 @@
     forward(1, grp, times[1])
     for c in range(chunks):
         span = pl.ds(c * LANES, LANES)
-        goal = to_row(arrived[c * LANES:(c + 1) * LANES, width:])
+        goal = to_row(arrived[c * LANES:(c + 1) * LANES])
         mine_part[1, grp, :, span] = mine_part[1, grp, :, span] - goal
 
     for s in range(1, groups):
-        across(s).wait_recv()
-
-        @pl.when(exists(here + near))
-        def _():
-            near_copy(s).start()
+        for k in range(2):
+            across(s, k).wait_recv()
+
+            @pl.when(exists(here + near))
+            def _():
+                near_copy(s, k).start()
 
         forward(1, source(s), times[1])
 
@@ -259,7 +278,8 @@
         for s in range(groups):
             @pl.when(exists(here + side))
             def _():
-                share(-side, s, source(s), grp).wait_recv()
+                for k in range(2):
+                    share(-side, s, source(s), grp, k).wait_recv()
 
             forward(1 + side, source(s), listed)
 
@@ -329,17 +349,20 @@
 
     repeat(tiles - 1, lambda step: first(step).wait_send())
     for s in range(1, groups):
-        across(s).wait_send()
+        for k in range(2):
+            across(s, k).wait_send()
 
     @pl.when(exists(here + near))
     def _():
         for s in range(groups):
-            near_copy(s).wait_send()
+            for k in range(2):
+                near_copy(s, k).wait_send()
 
     @pl.when(exists(here - near))
     def _():
         for s in range(groups):
-            far_copy(s).wait_send()
+            for k in range(2):
+                far_copy(s, k).wait_send()
 
     for d, s in spread:
         @pl.when(exists(here + d))
@@ -347,10 +370,17 @@
             third(d, s).wait_send()
 
 
-def finish(rows, means, scales, out_rows, out_means, out_scales):
-    out_rows[...] = rows[...]
-    out_means[...] = means[...]
-    out_scales[...] = scales[...]
+def finish(rows, means, scales, out_rows, out_means, out_scales, sems):
+    copies = [
+        pltpu.make_async_copy(source, target, sems.at[index])
+        for index, (source, target) in enumerate(
+            ((rows, out_rows), (means, out_means), (scales, out_scales))
+        )
+    ]
+    for copy in copies:
+        copy.start()
+    for copy in copies:
+        copy.wait()
 
 
 def shards(points, targets, morton, inducing, means, scales, neighbours):
@@ -366,9 +396,9 @@
     result = pl.pallas_call(
         functools.partial(kernel, tiles, groups),
         out_shape=(
-            jax.ShapeDtypeStruct((size, width), F32),
-            jax.ShapeDtypeStruct((1, size), F32),
-            jax.ShapeDtypeStruct((1, size), F32),
+            pltpu.VMEM((size, width), F32),
+            pltpu.VMEM((1, size), F32),
+            pltpu.VMEM((1, size), F32),
         ),
         in_specs=[pl.BlockSpec(memory_space=pltpu.HBM)] * 7,
         out_specs=(vmem, vmem, vmem),
@@ -391,7 +421,7 @@
             pltpu.VMEM(pair, F32),
             pltpu.VMEM((groups, 1, rows), F32),
             dma((tiles - 1,)), dma((tiles - 1,)),
-            dma((3, groups)), dma((3, groups)),
+            dma((3, groups, 2)), dma((3, groups, 2)),
             dma((5, groups)), dma((5, groups)),
         ],
         compiler_params=pltpu.CompilerParams(
@@ -405,7 +435,9 @@
         finish,
         out_shape=[jax.ShapeDtypeStruct(part.shape, F32) for part in result],
         in_specs=[vmem] * 3,
-        out_specs=[vmem] * 3,
+        out_specs=[pl.BlockSpec(memory_space=pl.ANY)] * 3,
+        scratch_shapes=[dma((3,))],
+        compiler_params=pltpu.CompilerParams(vmem_limit_bytes=4 << 20),
     )(*result)
     return result[0], result[1].reshape(size), result[2].reshape(size)
 

time: 22.9 us -> 20.8 us (0.908)
  Pallas kernels: 22.2 us -> 20 us
    pallas_call x1, Pallas kernels: 20.5 us -> 19.3 us  [shards(): pl.pallas_call(functools.partial(kernel, tiles, groups), out_shape=(pltpu...]
    pallas_call x1, Pallas kernels: 1.68 us -> 0.74 us  [shards(): pl.pallas_call(finish, out_shape=[jax.ShapeDtypeStruct(part.shape, F32) f...]
where the time goes in v3:
time: 20.8 us; the launch traced here: 20.6 us
  Pallas kernels  20 us (96%)
  between operations  0.64 us (3%)
    pallas_call x1, Pallas kernels, shards(): pl.pallas_call(functools.partial(kernel, tiles, groups), out_shape=(pltpu...  19.3 us
    pallas_call x1, Pallas kernels, shards(): pl.pallas_call(finish, out_shape=[jax.ShapeDtypeStruct(part.shape, F32) f...  0.74 us

profile of v3, /device:TPU:0, one launch (start us, length us, event | category | flops | bytes accessed | tf_op | source)
XLA Modules:
  0.0 20.6 jit_solution(16977754533892639959)
XLA Ops:
  0.6 19.3 %shard_map.94 = (f32[256,256]{1,0:T(8,128)S(1)}, f32[1,256]{1,0:T(1,128)S(1)}, f32[1,256]{1,0:T(1,128)S(1)}) custom-call(bf16[128,256]{1,0:T(8,128)(2,1)} %points_in.1, bf16[1,128]{1,0:T(2,128)(2,1)} %bitcast.10, s32[1,128]{1,0:T(1,128)} %bitcast.11, bf16[512,256]{1,0:T(8,128)(2,1)} %inducing_in.1, bf16[4,128]{1,0:T(4,128)(2,1)} %bitcast.8, ...), custom_call_target="tpu_custom_call" | custom-call | tf_op jit(solution)/shard_map/pallas_call | solution.py:396
  19.9 0.7 %shard_map.95 = (f32[256,256]{1,0:T(8,128)}, f32[1,256]{1,0:T(1,128)}, f32[1,256]{1,0:T(1,128)}) custom-call(f32[256,256]{1,0:T(8,128)S(1)} %get-tuple-element.9.rows, f32[1,256]{1,0:T(1,128)S(1)} %get-tuple-element.10.means, f32[1,256]{1,0:T(1,128)S(1)} %get-tuple-element.11.scales), custom_call_target="tpu_custom_call" | custom-call | tf_op jit(solution)/shard_map/pallas_call | solution.py:434

commit v4 on v3

--- a/solution.py
+++ b/solution.py
@@ -257,6 +257,27 @@
 
         repeat(chunks, piece)
 
+    def third(r, e, step):
+        d = r - 1 + e
+        return pltpu.make_async_remote_copy(
+            src_ref=mine_part.at[r], dst_ref=parts.at[2 - d, grp, r],
+            send_sem=send3.at[r, e + 1, step], recv_sem=recv3.at[r, e + 1, step],
+            device_id=(here + d, other(step)), device_id_type=MESH,
+        )
+
+    def publish(r):
+        for e in (1, -1, 0):
+            for step in range(groups):
+                d = r - 1 + e
+
+                @pl.when(exists(here + d) & ((d != 0) | (step != 0)))
+                def _():
+                    third(r, e, step).start()
+
+    spread = [
+        (r, e, s) for r in range(3) for e in range(-1, 2) for s in range(groups)
+        if (r - 1 + e, s) != (0, 0)
+    ]
     forward(1, grp, times[1])
     for c in range(chunks):
         span = pl.ds(c * LANES, LANES)
@@ -273,6 +294,7 @@
 
         forward(1, source(s), times[1])
 
+    publish(jnp.int32(1))
     for side in (near, -near):
         listed = jnp.where(side > 0, times[2], times[0])
         for s in range(groups):
@@ -282,25 +304,13 @@
                     share(-side, s, source(s), grp, k).wait_recv()
 
             forward(1 + side, source(s), listed)
-
-    def third(d, step):
-        return pltpu.make_async_remote_copy(
-            src_ref=mine_part, dst_ref=parts.at[2 - d, grp],
-            send_sem=send3.at[2 - d, step], recv_sem=recv3.at[2 - d, step],
-            device_id=(here + d, other(step)), device_id_type=MESH,
-        )
-
-    spread = [(d, s) for d in range(-2, 3) for s in range(groups) if (d, s) != (0, 0)]
-    for d, s in spread:
-        @pl.when(exists(here + d))
+        publish(1 + side)
+
+    parts[2, grp] = mine_part[...]
+    for r, e, s in spread:
+        @pl.when(exists(here - (r - 1 + e)))
         def _():
-            third(d, s).start()
-
-    parts[2, grp] = mine_part[...]
-    for d, s in spread:
-        @pl.when(exists(here - d))
-        def _():
-            third(d, s).wait_recv()
+            third(r, e, s).wait_recv()
 
     total_mean = jnp.zeros((size, 1), F32)
     total_scale = jnp.zeros((size, 1), F32)
@@ -364,10 +374,10 @@
             for k in range(2):
                 far_copy(s, k).wait_send()
 
-    for d, s in spread:
-        @pl.when(exists(here + d))
+    for r, e, s in spread:
+        @pl.when(exists(here + (r - 1 + e)))
         def _():
-            third(d, s).wait_send()
+            third(r, e, s).wait_send()
 
 
 def finish(rows, means, scales, out_rows, out_means, out_scales, sems):
@@ -422,7 +432,7 @@
             pltpu.VMEM((groups, 1, rows), F32),
             dma((tiles - 1,)), dma((tiles - 1,)),
             dma((3, groups, 2)), dma((3, groups, 2)),
-            dma((5, groups)), dma((5, groups)),
+            dma((3, 3, groups)), dma((3, 3, groups)),
         ],
         compiler_params=pltpu.CompilerParams(
             collective_id=0, has_side_effects=True, vmem_limit_bytes=62 << 20

time: 20.8 us -> 21 us (level)
  no operation moved by 1% of the time
where the time goes in v4:
time: 21 us; the launch traced here: 20.8 us
  Pallas kernels  20.2 us (96%)
  between operations  0.64 us (3%)
    pallas_call x1, Pallas kernels, shards(): pl.pallas_call(functools.partial(kernel, tiles, groups), out_shape=(pltpu...  19.5 us
    pallas_call x1, Pallas kernels, shards(): pl.pallas_call(finish, out_shape=[jax.ShapeDtypeStruct(part.shape, F32) f...  0.74 us

profile of v4, /device:TPU:0, one launch (start us, length us, event | category | flops | bytes accessed | tf_op | source)
XLA Modules:
  0.0 20.8 jit_solution(7207660551642366272)
XLA Ops:
  0.6 19.5 %shard_map.94 = (f32[256,256]{1,0:T(8,128)S(1)}, f32[1,256]{1,0:T(1,128)S(1)}, f32[1,256]{1,0:T(1,128)S(1)}) custom-call(bf16[128,256]{1,0:T(8,128)(2,1)} %points_in.1, bf16[1,128]{1,0:T(2,128)(2,1)} %bitcast.10, s32[1,128]{1,0:T(1,128)} %bitcast.11, bf16[512,256]{1,0:T(8,128)(2,1)} %inducing_in.1, bf16[4,128]{1,0:T(4,128)(2,1)} %bitcast.8, ...), custom_call_target="tpu_custom_call" | custom-call | tf_op jit(solution)/shard_map/pallas_call | solution.py:406
  20.1 0.7 %shard_map.95 = (f32[256,256]{1,0:T(8,128)}, f32[1,256]{1,0:T(1,128)}, f32[1,256]{1,0:T(1,128)}) custom-call(f32[256,256]{1,0:T(8,128)S(1)} %get-tuple-element.9.rows, f32[1,256]{1,0:T(1,128)S(1)} %get-tuple-element.10.means, f32[1,256]{1,0:T(1,128)S(1)} %get-tuple-element.11.scales), custom_call_target="tpu_custom_call" | custom-call | tf_op jit(solution)/shard_map/pallas_call | solution.py:444
